TPU v7x, 256 devices: a whole 4x4x8 slice. The times are simulated.
256 devices in a mesh: seq: 32 (over z, x), head: 8 (over y, core).
Axes of the slice: x: 4, y: 4, z: 8, core: 2. Of those that a mesh axis runs over, the one named last changes fastest.
Arguments:
- mixer_input: bfloat16 [65536, 5120], P('seq', 'head'), may hold values from -6 to 6
- write_rows: bfloat16 [65536, 128], P(('seq', 'head')), may hold values from -1.796875 to 1.796875
- read_rows: bfloat16 [65536, 128], P(('seq', 'head')), may hold values from -1.796875 to 1.796875
- log_decay: float32 [80, 65536], P('head', 'seq'), may hold values from -2 to 0, as said below
- skip_gain: float32 [80], P('head'), may hold values from 0.25 to 1.75
- reset_offsets: int32 [32, 4], P('seq'), may hold values from 0 to 2048, as said below
- grad_out: bfloat16 [65536, 5120], P('seq', 'head'), may hold values from -6 to 6
Outputs:
- grad_input: bfloat16 [65536, 5120], P('seq', 'head')
- grad_write: float32 [65536, 128], P(('seq', 'head'))
- grad_read: float32 [65536, 128], P(('seq', 'head'))
Inputs may be any that keep to these rules, and one draw needn't show every extreme that they name: `log_decay`: every entry is negative. `reset_offsets`: row d lists, in increasing order, the offsets within block d of 2048 tokens at which an episode begins; unused slots hold 2048 and stand after the used ones; some row uses all 4 slots.
All inputs are finite; a program needn't handle non-finite values.
Results may differ from a plain program's by a relative error of at most 0.0055.
Values may be sent and summed in bfloat16 or wider, within the bound.
No kernel may reach another device: no remote copies, remote signals or barrier semaphores. Data moves between devices by JAX's collectives and lax.ppermute only.
A program may use at most 192 MiB of HBM per device.

v0:
```python
import jax
import jax.numpy as jnp
from jax import lax
from jax.sharding import PartitionSpec as P

SPAN = 256


def entering(part, axis, combine, identity, reverse):
    count = lax.axis_size(axis)
    place = lax.axis_index(axis)
    ahead = count - 1 - place if reverse else place
    gathered = jax.tree.map(lambda a: lax.all_gather(a, axis), part)
    state = jax.tree.map(lambda a, e: jnp.zeros_like(a) + jnp.asarray(e, a.dtype), part, identity)

    def one(step, state):
        source = count - 1 - step if reverse else step
        return combine(
            state, jax.tree.map(lambda a: lax.dynamic_index_in_dim(a, source, 0, False), gathered)
        )

    return lax.fori_loop(0, ahead, one, state)


def span_update(carry_state, inputs, skip_gain):
    feature_part, write_part, read_part, log_part, reset_part = inputs
    span_len = reset_part.shape[0]
    cum_log = jnp.cumsum(log_part, axis=1)
    reset_count = jnp.cumsum(reset_part)
    input_gain = jnp.sqrt(-jnp.expm1(2.0 * log_part))
    positions = jnp.arange(span_len)
    allowed = (positions[:, None] >= positions[None, :]) & (
        reset_count[:, None] == reset_count[None, :]
    )
    spread = cum_log[:, :, None] - cum_log[:, None, :]
    decay_matrix = jnp.exp(jnp.where(allowed[None], spread, -1e30))
    scores = jnp.dot(read_part, write_part.T, precision=lax.Precision.HIGHEST)
    weights = decay_matrix * scores[None] * input_gain[:, None, :]
    result = jnp.einsum("hts,shp->thp", weights, feature_part, precision=lax.Precision.HIGHEST)
    entry_decay = jnp.exp(cum_log) * (reset_count == 0)[None, :]
    carried = jnp.einsum("tn,hnp->thp", read_part, carry_state, precision=lax.Precision.HIGHEST)
    result = result + carried * entry_decay.T[:, :, None] + skip_gain[None, :, None] * feature_part
    tail_weight = (
        jnp.exp(cum_log[:, -1:] - cum_log) * (reset_count == reset_count[-1])[None, :] * input_gain
    )
    block_decay = jnp.exp(cum_log[:, -1]) * (reset_count[-1] == 0)
    fresh_state = jnp.einsum(
        "sn,shp->hnp",
        write_part,
        feature_part * tail_weight.T[:, :, None],
        precision=lax.Precision.HIGHEST,
    )
    return (block_decay[:, None, None] * carry_state + fresh_state, result)


def link_states(earlier, later):
    return (earlier[0] * later[0], later[0][:, None, None] * earlier[1] + later[1])


def shards(mixer_input, write_rows, read_rows, log_decay, skip_gain, reset_offsets, grad_out):
    write_whole, read_whole = (
        lax.all_gather(write_rows, "head", axis=0, tiled=True),
        lax.all_gather(read_rows, "head", axis=0, tiled=True),
    )
    token_count = mixer_input.shape[0]
    head_count = log_decay.shape[0]
    head_width = mixer_input.shape[1] // head_count
    feature_full = mixer_input.astype(jnp.float32).reshape(token_count, head_count, head_width)
    write_full = write_whole.astype(jnp.float32)
    read_full = read_whole.astype(jnp.float32)
    cotangent = grad_out.astype(jnp.float32).reshape(token_count, head_count, head_width)
    positions = jnp.arange(token_count, dtype=jnp.int32)
    resets = jnp.any(positions[:, None] == reset_offsets[0][None, :], axis=1).astype(jnp.float32)
    cum_log = jnp.cumsum(log_decay, axis=1)
    reset_count = jnp.cumsum(resets)
    input_gain = jnp.sqrt(-jnp.expm1(2.0 * log_decay))
    tail_weight = (
        jnp.exp(cum_log[:, -1:] - cum_log) * (reset_count == reset_count[-1])[None, :] * input_gain
    )
    local_state = jnp.einsum(
        "tn,thp->hnp",
        write_full,
        feature_full * tail_weight.T[:, :, None],
        precision=lax.Precision.HIGHEST,
    )
    block_decay = jnp.exp(cum_log[:, -1]) * (reset_count[-1] == 0)
    entry_decay = jnp.exp(cum_log) * (reset_count == 0)[None, :]
    local_grad = jnp.einsum(
        "tn,thp->hnp",
        read_full,
        cotangent * entry_decay.T[:, :, None],
        precision=lax.Precision.HIGHEST,
    )
    identity = (jnp.ones_like(block_decay), jnp.zeros_like(local_state))
    decay_before, state_in = entering(
        (block_decay, local_state), "seq", link_states, identity, False
    )
    decay_after, grad_in = entering((block_decay, local_grad), "seq", link_states, identity, True)
    spans = token_count // SPAN
    log_blocks = log_decay.reshape(head_count, spans, SPAN).transpose(1, 0, 2)
    reset_blocks = resets.reshape(spans, SPAN)

    def block_forward(feature_arg, write_arg, read_arg):
        feature_blocks = feature_arg.reshape(spans, SPAN, head_count, head_width)
        write_blocks = write_arg.reshape(spans, SPAN, write_arg.shape[1])
        read_blocks = read_arg.reshape(spans, SPAN, read_arg.shape[1])

        def advance(carry_state, inputs):
            return span_update(carry_state, inputs, skip_gain)

        end_state, outputs = lax.scan(
            advance, state_in, (feature_blocks, write_blocks, read_blocks, log_blocks, reset_blocks)
        )
        return (outputs.reshape(token_count, head_count, head_width), end_state)

    outputs, pullback = jax.vjp(block_forward, feature_full, write_full, read_full)
    grad_feature, grad_write_all, grad_read_all = pullback((cotangent, grad_in))
    grad_write, grad_read = (
        lax.psum_scatter(grad_write_all, "head", scatter_dimension=0, tiled=True),
        lax.psum_scatter(grad_read_all, "head", scatter_dimension=0, tiled=True),
    )
    grad_input = grad_feature.reshape(token_count, head_count * head_width).astype(jnp.bfloat16)
    return (grad_input, grad_write, grad_read)


def solution(mesh):
    in_specs = (
        P("seq", "head"),
        P(("seq", "head"), None),
        P(("seq", "head"), None),
        P("head", "seq"),
        P("head"),
        P("seq", None),
        P("seq", "head"),
    )
    out_specs = (P("seq", "head"), P(("seq", "head"), None), P(("seq", "head"), None))
    return jax.shard_map(shards, mesh=mesh, in_specs=in_specs, out_specs=out_specs, check_vma=False)
```

profile of v0, /device:TPU:4, one launch (start us, length us, event | category | flops | bytes accessed | tf_op | source)
XLA Modules:
  0.0 574.7 jit_solution(11024643300926106177)
XLA Ops:
  18.5 13.6 %all_gather.28 = bf16[2048,128]{1,0:T(8,128)(2,1)S(1)} all-gather(bf16[256,128]{1,0:T(8,128)(2,1)S(1)} %copy-done.5), channel_id=1, replica_groups=mesh['seq'=32,'head'=8] {'head'}, dimensions={0}, use_global_device_ids=true | all-gather | bytes 589824 | tf_op jit(solution)/shard_map/all_gather | solution.py:62
  40.3 13.2 %all_gather.25 = bf16[2048,128]{1,0:T(8,128)(2,1)S(1)} all-gather(bf16[256,128]{1,0:T(8,128)(2,1)S(1)} %copy-done.6), channel_id=1, replica_groups=mesh['seq'=32,'head'=8] {'head'}, dimensions={0}, use_global_device_ids=true | all-gather | bytes 589824 | tf_op jit(solution)/shard_map/all_gather | solution.py:63
  60.3 74.4 %all-reduce = f32[320]{0:T(512)S(1)} all-reduce(f32[320]{0:T(512)S(1)} %dynamic-update-slice), channel_id=2, replica_groups=mesh['seq'=32,'head'=8] {'seq'}, use_global_device_ids=true, to_apply=%add | all-reduce | flops 320 | bytes 2560
  134.8 5.0 copy.94
  144.9 7.4 %copy.95 = f32[80,8,8,256]{3,2,1,0:T(8,128)} copy(f32[80,8,8,256]{3,1,2,0:T(8,128)} %bitcast.375) | data formatting | bytes 10485760
  155.5 115.7 %while.83 = (s32[]{:T(128)}, f32[10,128,64]{1,2,0:T(8,128)S(1)}, f32[8,128,256]{1,2,0:T(8,128)}, f32[8,10,256,256]{3,2,1,0:T(8,128)}, f32[8,10,1,256]{3,1,2,0:T(...) while((s32[]{:T(128)}, f32[10,128,64]{1,2,0:T(8,128)S(1)}, ...), condition=%wide.region_14.15_spmd.clone.clone, body=%wide.region_9.14_spmd.clone.sunk.clone | while | flops 356031040 | bytes 10219655 | solution.py:111
  271.2 42.5 %while.80 = (s32[]{:T(128)}, f32[10,128,64]{2,1,0:T(8,128)S(1)}, s32[]{:T(128)}, f32[32,10]{1,0:T(8,128)S(1)}, f32[32,10,128,64]{2,3,1,0:T(8,128)}) while((s32[]{:T(128)}, f32[10,128,64]{2,1,0:T(8,128)S(1)}, s32[]{:T(128)}, f32[32,10]{1,0:T(8,128)S(1)}, f32[32,10,128,64]{2,3,1,0:T(8,128)}) %tuple.184), condition=%wide.region_6.7_spmd.clone, body=%wide.region_5.6_spmd.sunk.clone | while | flops 163846 | bytes 2293995 | solution.py:22
  315.1 182.8 %while.82 = (s32[]{:T(128)}, f32[10,128,64]{1,2,0:T(8,128)S(1)}, bf16[8,256,10,64]{1,3,2,0:T(8,128)(2,1)}, f32[8,256,128]{2,1,0:T(8,128)S(1)}, f32[8,256,128]{2,...) while((s32[]{:T(128)}, f32[10,128,64]{1,2,0:T(8,128)S(1)}, ...), condition=%wide.region_17.18_spmd.clone, body=%wide.region_15.17_spmd.sunk.clone | while | flops 2217705472 | bytes 16956240 | solution.py:111
  319.6 4.2 fusion.184
  323.8 4.4 fusion.185
  346.7 4.4 fusion.185
  365.3 4.2 fusion.184
  369.5 4.4 fusion.185
  392.3 4.4 fusion.185
  411.0 4.2 fusion.184
  415.2 4.4 fusion.185
  433.8 4.2 fusion.184
  438.0 4.4 fusion.185
  456.7 4.2 fusion.184
  460.9 4.4 fusion.185
  479.5 4.2 fusion.184
  483.8 4.4 fusion.185
  506.3 25.5 %reduce-scatter.3.cloned.1.call-done = f32[256,128]{1,0:T(8,128)} async-done(((f32[2048,128]{1,0:T(8,128)}), f32[256,128]{1,0:T(8,128)}) %reduce-scatter.3.cloned.1.call-update) | async-done | bytes 131088 | tf_op jit(solution)/shard_map/reduce_scatter | solution.py:119
  531.9 36.3 %reduce-scatter.5.cloned.1.call-done = f32[256,128]{1,0:T(8,128)} async-done(((f32[2048,128]{1,0:T(8,128)}), f32[256,128]{1,0:T(8,128)}) %reduce-scatter.5.cloned.1.call-update) | async-done | bytes 131088 | tf_op jit(solution)/shard_map/reduce_scatter | solution.py:120
  (545 shorter events, 317.8 us)
Async XLA Ops:
  7.2 145.1 %all-gather.8.cloned.1.call-start = ((), (), s32[]{:S(2)}) async-start(), calls=%async_computation.5 | async-start | bytes 10813440 | tf_op jit(solution)/shard_map/all_gather | solution.py:13
  14.8 3.7 copy-start.5
  17.8 14.5 %copy-start.3 = (f32[10,2048]{1,0:T(8,128)S(1)}, f32[10,2048]{1,0:T(8,128)}, u32[]{:S(2)}) copy-start(f32[10,2048]{1,0:T(8,128)} %param.18) | copy-start | bytes 245764
  18.5 14.6 %copy-start = (f32[2048,640]{0,1:T(8,128)}, f32[2048,640]{0,1:T(8,128)S(1)}, u32[]{:S(2)}) copy-start(f32[2048,640]{0,1:T(8,128)S(1)} %convert_element_type.76) | copy-start | bytes 15728644
  36.5 3.8 copy-start.6
  36.5 234.6 %all-gather.6.cloned.1.call-start = ((), (), s32[]{:S(2)}) async-start(), calls=%async_computation.4 | async-start | bytes 10813440 | tf_op jit(solution)/shard_map/all_gather | solution.py:13
  39.5 14.0 %copy-start.4 = (f32[2048,10]{0,1:T(8,128)S(1)}, f32[2048,10]{0,1:T(8,128)}, u32[]{:S(2)}) copy-start(f32[2048,10]{0,1:T(8,128)} %get-tuple-element.1043) | copy-start | bytes 245764
  40.2 13.3 %copy-start.1 = (f32[2048,640]{0,1:T(8,128)}, f32[2048,640]{0,1:T(8,128)S(1)}, u32[]{:S(2)}) copy-start(f32[2048,640]{0,1:T(8,128)S(1)} %convert_element_type.74) | copy-start | bytes 15728644
  40.2 18.5 %copy-start.8 = (u32[256]{0:T(256)S(1)}, u32[256]{0:T(256)}, u32[]{:S(2)}) copy-start(u32[256]{0:T(256)} %constant.201) | copy-start | bytes 3076
  56.8 475.0 %reduce-scatter.3.cloned.1.call-start = ((), (), s32[]{:S(2)}) async-start(), calls=%async_computation.2 | async-start | bytes 1179648 | tf_op jit(solution)/shard_map/reduce_scatter | solution.py:119
  271.2 43.9 %copy-start.7 = (f32[10]{0:T(128)S(1)}, f32[10]{0:T(128)}, u32[]{:S(2)}) copy-start(f32[10]{0:T(128)} %param.19) | copy-start | bytes 124
  497.9 1.0 copy-start.2
  498.9 69.3 %reduce-scatter.5.cloned.1.call-start = ((), (), s32[]{:S(2)}) async-start(), calls=%async_computation.3 | async-start | bytes 1179648 | tf_op jit(solution)/shard_map/reduce_scatter | solution.py:120
Sparse Core Ops, SparseCore 0:
  36.6 110.4 all-gather.7
  149.7 105.9 all-gather.5
  499.0 32.8 reduce-scatter.2
  534.8 33.3 reduce-scatter.4
where the time goes:
time: 579 us; the launch traced here: 575 us
  matrix products  184 us (32%)
  local copies, waits for them, and re-layouts  124 us (21%)
  blocking collectives  101 us (17%)
  other arithmetic  78.9 us (14%)
  waiting for transfers between devices  62.2 us (11%)
  between operations  15.4 us (3%)
  loops' own time  8.71 us (2%)
    unnamed x1, blocking collectives  74.4 us
    dot_general x16, matrix products, span_update(): jnp.einsum('hts,shp->thp', weights, feature_part, precision=lax.Precision...  68.6 us
    dynamic_update_slice x32, other arithmetic, block_forward(): lax.scan(advance, state_in, (feature_blocks, write_blocks, read_blocks, l...  45.9 us
    dot_general x24, matrix products, span_update(): jnp.einsum('sn,shp->hnp', write_part, feature_part * tail_weight.T[:, :,...  39.4 us
    dynamic_slice x62, local copies, waits for them, and re-layouts, one(): lax.dynamic_index_in_dim(a, source, 0, False)  38.2 us
    dot_general x24, matrix products, span_update(): scores = jnp.dot(read_part, write_part.T, precision=lax.Precision.HIGHEST)  37.9 us
    reduce_scatter x1, waiting for transfers between devices, shards(): lax.psum_scatter(grad_read_all, 'head', scatter_dimension=0, tiled=True)  36.3 us
    dot_general x16, matrix products, span_update(): jnp.einsum('tn,hnp->thp', read_part, carry_state, precision=lax.Precision...  31.6 us
  transfers between devices with their start and end apart: 4, of which 2 were waited for; matrix products, arithmetic and copies ran while one was open for 25% of the time, Pallas kernels for 0%

commit v1 on v0

--- a/solution.py
+++ b/solution.py
@@ -59,7 +59,9 @@
 
 def shards(mixer_input, write_rows, read_rows, log_decay, skip_gain, reset_offsets, grad_out):
     write_whole, read_whole = (
-        lax.all_gather(write_rows, "head", axis=0, tiled=True),
+        jnp.concatenate(
+            lax.all_to_all(jnp.stack([write_rows] * lax.axis_size("head")), "head", 0, 0), axis=0
+        ),
         lax.all_gather(read_rows, "head", axis=0, tiled=True),
     )
     token_count = mixer_input.shape[0]

time: 579 us -> 690 us (1.19)
  waiting for transfers between devices: 62.2 us -> 163 us
  blocking collectives: 101 us -> 88.2 us
  local copies, waits for them, and re-layouts: 124 us -> 134 us
    all_gather x2, waiting for transfers between devices: 0.01 us -> 56.1 us  [entering(): gathered = jax.tree.map(lambda a: lax.all_gather(a, axis), part)]
    reduce_scatter x1, waiting for transfers between devices: 25.5 us -> 65.7 us  [shards(): lax.psum_scatter(grad_write_all, 'head', scatter_dimension=0, tiled=True)]
    all_gather x1 -> x0, blocking collectives: 13.6 us -> none  [shards(): lax.all_gather(write_rows, 'head', axis=0, tiled=True)]
    unnamed x33 -> x31, local copies, waits for them, and re-layouts: 28.9 us -> 30.1 us
  transfers between devices with their start and end apart: 4 -> 5, of which waited for: 2 -> 4; matrix products, arithmetic and copies ran while one was open for 25% -> 12% of each run, Pallas kernels for 0% -> 0%
where the time goes in v1:
time: 690 us; the launch traced here: 685 us
  matrix products  186 us (27%)
  waiting for transfers between devices  163 us (24%)
  local copies, waits for them, and re-layouts  134 us (19%)
  blocking collectives  88.2 us (13%)
  other arithmetic  85.3 us (12%)
  between operations  15.4 us (2%)
  loops' own time  8.52 us (1%)
    unnamed x1, blocking collectives  74.3 us
    dot_general x16, matrix products, span_update(): jnp.einsum('hts,shp->thp', weights, feature_part, precision=lax.Precision...  68.5 us
    reduce_scatter x1, waiting for transfers between devices, shards(): lax.psum_scatter(grad_write_all, 'head', scatter_dimension=0, tiled=True)  65.7 us
    all_gather x2, waiting for transfers between devices, entering(): gathered = jax.tree.map(lambda a: lax.all_gather(a, axis), part)  56.1 us
    dynamic_update_slice x32, other arithmetic, block_forward(): lax.scan(advance, state_in, (feature_blocks, write_blocks, read_blocks, l...  45.8 us
    dot_general x24, matrix products, span_update(): jnp.einsum('sn,shp->hnp', write_part, feature_part * tail_weight.T[:, :,...  39.3 us
    dynamic_slice x62, local copies, waits for them, and re-layouts, one(): lax.dynamic_index_in_dim(a, source, 0, False)  38.3 us
    dot_general x24, matrix products, span_update(): scores = jnp.dot(read_part, write_part.T, precision=lax.Precision.HIGHEST)  37.8 us
  transfers between devices with their start and end apart: 5, of which 4 were waited for; matrix products, arithmetic and copies ran while one was open for 12% of the time, Pallas kernels for 0%

profile of v1, /device:TPU:4, one launch (start us, length us, event | category | flops | bytes accessed | tf_op | source)
XLA Modules:
  0.0 685.1 jit_solution(9586723761965164528)
XLA Ops:
  15.4 13.8 %all_gather.22 = bf16[2048,128]{1,0:T(8,128)(2,1)S(1)} all-gather(bf16[256,128]{1,0:T(8,128)(2,1)} %param.17), channel_id=1, replica_groups=mesh['seq'=32,'head'=8] {'head'}, dimensions={0}, use_global_device_ids=true | all-gather | bytes 589824 | tf_op jit(solution)/shard_map/all_gather | solution.py:65
  49.7 4.3 all-to-all-done
  54.0 5.8 convolution_bitcast_fusion.4
  64.4 74.3 %all-reduce = f32[320]{0:T(512)S(1)} all-reduce(f32[320]{0:T(512)S(1)} %dynamic-update-slice), channel_id=2, replica_groups=mesh['seq'=32,'head'=8] {'seq'}, use_global_device_ids=true, to_apply=%add | all-reduce | flops 320 | bytes 2560
  138.8 5.0 copy.95
  148.8 7.4 %copy.96 = f32[80,8,8,256]{3,2,1,0:T(8,128)} copy(f32[80,8,8,256]{3,1,2,0:T(8,128)} %bitcast.375) | data formatting | bytes 10485760
  159.2 42.3 %while.80 = (s32[]{:T(128)}, f32[10,128,64]{2,1,0:T(8,128)S(1)}, s32[]{:T(128)}, f32[32,10]{1,0:T(8,128)S(1)}, f32[32,10,128,64]{2,3,1,0:T(8,128)}) while((s32[]{:T(128)}, f32[10,128,64]{2,1,0:T(8,128)S(1)}, s32[]{:T(128)}, f32[32,10]{1,0:T(8,128)S(1)}, f32[32,10,128,64]{2,3,1,0:T(8,128)}) %tuple.183), condition=%wide.region_6.7_spmd.clone, body=%wide.region_5.6_spmd.sunk.clone | while | flops 163846 | bytes 2293995 | solution.py:22
  201.7 56.0 %all-gather.8.cloned.1.call-done = f32[320,128,64]{1,2,0:T(8,128)} async-done(((f32[10,128,64]{1,2,0:T(8,128)}), f32[320,128,64]{1,2,0:T(8,128)}) %all-gather.8.cloned.1.call-update) | async-done | bytes 10485776 | tf_op jit(solution)/shard_map/all_gather | solution.py:13
  261.0 118.4 %while.83 = (s32[]{:T(128)}, f32[10,128,64]{1,2,0:T(8,128)S(1)}, f32[8,128,256]{1,2,0:T(8,128)}, f32[8,10,256,256]{3,2,1,0:T(8,128)}, f32[8,10,1,256]{3,1,2,0:T(...) while((s32[]{:T(128)}, f32[10,128,64]{1,2,0:T(8,128)S(1)}, ...), condition=%wide.region_14.15_spmd.clone.clone, body=%wide.region_9.14_spmd.clone.sunk.clone | while | flops 356031040 | bytes 10226307 | solution.py:113
  380.5 187.7 %while.82 = (s32[]{:T(128)}, f32[10,128,64]{1,2,0:T(8,128)S(1)}, bf16[8,256,10,64]{1,3,2,0:T(8,128)(2,1)}, f32[8,256,128]{2,1,0:T(8,128)S(1)}, f32[8,256,128]{2,...) while((s32[]{:T(128)}, f32[10,128,64]{1,2,0:T(8,128)S(1)}, ...), condition=%wide.region_17.18_spmd.clone, body=%wide.region_15.17_spmd.sunk.clone | while | flops 2217705472 | bytes 16956240 | solution.py:113
  385.0 4.2 fusion.179
  389.2 4.4 fusion.180
  408.4 4.2 fusion.179
  412.6 4.4 fusion.180
  436.1 4.4 fusion.180
  459.6 4.4 fusion.180
  483.0 4.4 fusion.180
  506.4 4.4 fusion.180
  525.6 4.2 fusion.179
  529.8 4.4 fusion.180
  549.0 4.2 fusion.179
  553.2 4.4 fusion.180
  576.7 65.7 %reduce-scatter.3.cloned.1.call-done = f32[256,128]{1,0:T(8,128)} async-done(((f32[2048,128]{1,0:T(8,128)}), f32[256,128]{1,0:T(8,128)}) %reduce-scatter.3.cloned.1.call-update) | async-done | bytes 131088 | tf_op jit(solution)/shard_map/reduce_scatter | solution.py:121
  642.4 36.2 %reduce-scatter.5.cloned.1.call-done = f32[256,128]{1,0:T(8,128)} async-done(((f32[2048,128]{1,0:T(8,128)}), f32[256,128]{1,0:T(8,128)}) %reduce-scatter.5.cloned.1.call-update) | async-done | bytes 131088 | tf_op jit(solution)/shard_map/reduce_scatter | solution.py:122
  (546 shorter events, 343.8 us)
Async XLA Ops:
  7.2 152.0 %all-gather.6.cloned.1.call-start = ((), (), s32[]{:S(2)}) async-start(), calls=%async_computation.5 | async-start | bytes 10813440 | tf_op jit(solution)/shard_map/all_gather | solution.py:13
  32.2 1.6 copy-start.2
  32.9 2.4 copy-start
  32.9 5.7 copy-start.3
  39.5 14.5 %all-to-all-start = ((bf16[8,256,128]{2,1,0:T(8,128)(2,1)}), bf16[8,256,128]{2,1,0:T(8,128)(2,1)}, u32[]{:S(2)}, u32[]{:S(2)}) async-start(bf16[8,256,128]{2,1,0:T(8,128)(2,1)} %stack.2), calls=%async_computation | async-start | bytes 1048576 | tf_op jit(solution)/shard_map/all_to_all | solution.py:63
  43.6 214.2 %all-gather.8.cloned.1.call-start = ((), (), s32[]{:S(2)}) async-start(), calls=%async_computation.6 | async-start | bytes 10813440 | tf_op jit(solution)/shard_map/all_gather | solution.py:13
  59.8 3.1 copy-start.7
  59.8 4.3 copy-start.6
  59.8 582.6 %reduce-scatter.3.cloned.1.call-start = ((), (), s32[]{:S(2)}) async-start(), calls=%async_computation.3 | async-start | bytes 1179648 | tf_op jit(solution)/shard_map/reduce_scatter | solution.py:121
  143.8 4.9 copy-start.4
  261.0 119.5 %copy-start.5 = (f32[10]{0:T(128)S(1)}, f32[10]{0:T(128)}, u32[]{:S(2)}) copy-start(f32[10]{0:T(128)} %param.19) | copy-start | bytes 124
  568.2 1.0 copy-start.1
  569.3 109.4 %reduce-scatter.5.cloned.1.call-start = ((), (), s32[]{:S(2)}) async-start(), calls=%async_computation.4 | async-start | bytes 1179648 | tf_op jit(solution)/shard_map/reduce_scatter | solution.py:122
Sparse Core Ops, SparseCore 0:
  38.7 110.5 all-gather.5
  151.8 105.8 all-gather.7
  569.4 72.9 reduce-scatter.2
  645.3 33.2 reduce-scatter.4
